TPU v7x, 32 devices: a whole 2x2x4 slice. The times are simulated.
32 devices in a mesh: dev: 8 (over y, x, core), rep: 4 (over z).
Axes of the slice: x: 2, y: 2, z: 4, core: 2. Of those that a mesh axis runs over, the one named last changes fastest.
Arguments:
- backbone: bfloat16 [32, 16, 8, 512], P(('rep', 'dev')), parts along dimension 0, may hold values from -6 to 6
- conv_weight: bfloat16 [3, 3, 512, 2048], P(None, None, None, ('rep', 'dev')), parts along dimension 3, may hold values from -0.35355339 to 0.35355339
- smooth_weight: float32 [3, 3, 2048], P(None, None, 'rep'), parts along dimension 2, may hold values from -2.5 to 2.5
Outputs:
- smoothed: bfloat16 [32, 16, 8, 512], P(('rep', 'dev')), parts along dimension 0
There are 4 independent parts, one for each index of `rep`. A program takes and returns all parts, laid end to end along the dimension named above; each array names one. Nothing has to cross between parts.
All inputs are finite; a program needn't handle non-finite values.
Results may differ from a plain program's by a relative error of at most 0.0073.
Values may be sent and summed in bfloat16 or wider, within the bound.
A program may use at most 64 MiB of HBM per device.

v0:
```python
import jax
import jax.numpy as jnp
from jax import lax
from jax.sharding import PartitionSpec as P

ITERS = 2


ridge_term = 0.5


def convolve(padded, weights, grid_rows, grid_cols):
    summed = None
    for row_tap in range(3):
        for col_tap in range(3):
            window = padded[:, row_tap : row_tap + grid_rows, col_tap : col_tap + grid_cols, :]
            flat_window = window.reshape(-1, window.shape[3])
            product = jnp.dot(
                flat_window, weights[row_tap, col_tap], preferred_element_type=jnp.float32
            )
            summed = product if summed is None else summed + product
    return summed.reshape(padded.shape[0], grid_rows, grid_cols, weights.shape[3])


def single_root(moments):
    identity = jnp.eye(moments.shape[0], dtype=jnp.float32)
    frob = jnp.sqrt(jnp.sum(moments * moments))
    upper = moments / frob
    lower = identity
    for sweep in range(ITERS):
        product = jnp.dot(lower, upper, precision=lax.Precision.HIGHEST)
        factor = 1.5 * identity - 0.5 * product
        if sweep + 1 < ITERS:
            upper = jnp.dot(upper, factor, precision=lax.Precision.HIGHEST)
        lower = jnp.dot(factor, lower, precision=lax.Precision.HIGHEST)
    return lower / jnp.sqrt(frob)


def whiten_block(received):
    features_block = received[:, 0]
    image_count = features_block.shape[0]
    channels = features_block.shape[2]
    identity = jnp.eye(channels, dtype=jnp.float32)
    center = jnp.sum(features_block.astype(jnp.float32), axis=0) / image_count
    centered = (features_block.astype(jnp.float32) - center).astype(jnp.bfloat16)
    gram = jnp.einsum("nkc,nkd->kcd", centered, centered, preferred_element_type=jnp.float32)
    moments = gram / (image_count - 1) + ridge_term * identity
    roots = lax.map(single_root, moments)
    roots = roots.astype(jnp.bfloat16)
    whitened = jnp.einsum(
        "nkc,kcd->nkd", centered, roots, preferred_element_type=jnp.float32
    ).astype(jnp.bfloat16)
    return whitened[:, None]


def shards(backbone, conv_weight, smooth_weight):
    local_images = backbone.shape[0]
    grid_rows = backbone.shape[1]
    grid_cols = backbone.shape[2]
    channels = backbone.shape[3]
    owners = lax.axis_size("dev")
    padded = jnp.pad(backbone, ((0, 0), (1, 1), (1, 1), (0, 0)))
    kernel = lax.all_gather(conv_weight, "dev", axis=3, tiled=True)
    conv_out = convolve(padded, kernel, grid_rows, grid_cols)
    per_owner = grid_rows * grid_cols // owners
    features = conv_out.astype(jnp.bfloat16).reshape(local_images, owners, per_owner, channels)
    whitened = whiten_block(
        lax.all_to_all(features, "dev", split_axis=1, concat_axis=0, tiled=True)
    )
    returned = lax.all_to_all(whitened, "dev", split_axis=0, concat_axis=1, tiled=True)
    returned = returned.reshape(local_images, grid_rows, grid_cols, channels)
    padded_white = jnp.pad(returned, ((0, 0), (1, 1), (1, 1), (0, 0)))
    summed = jnp.zeros((local_images, grid_rows, grid_cols, channels), jnp.float32)
    for row_tap in range(3):
        for col_tap in range(3):
            window = padded_white[
                :, row_tap : row_tap + grid_rows, col_tap : col_tap + grid_cols, :
            ]
            summed = summed + window.astype(jnp.float32) * smooth_weight[row_tap, col_tap]
    return summed.astype(jnp.bfloat16)


def solution(mesh):
    placed = (
        P(("rep", "dev"), None, None, None),
        P(None, None, None, ("rep", "dev")),
        P(None, None, "rep"),
    )
    return jax.shard_map(
        shards,
        mesh=mesh,
        in_specs=placed,
        out_specs=P(("rep", "dev"), None, None, None),
        check_vma=False,
    )
```

profile of v0, /device:TPU:0, one launch (start us, length us, event | category | flops | bytes accessed | tf_op | source)
XLA Modules:
  0.0 323.5 jit_solution(15585913375034094981)
XLA Ops:
  7.3 43.6 %all-gather.2.cloned.1.call-done = bf16[3,3,512,512]{2,3,1,0:T(8,128)(2,1)} async-done(((bf16[3,3,512,64]{2,3,1,0:T(8,128)(2,1)}), bf16[3,3,512,512]{2,3,1,0:T(8,128)(2,1)}) %all-gather.2.cloned.1.call-update) | async-done | bytes 4718608 | tf_op jit(solution)/shard_map/all_gather | solution.py:63
  64.3 3.4 %all-to-all-start = ((bf16[1,8,16,512]{3,2,0,1:T(8,128)(2,1)}), bf16[1,8,16,512]{3,2,0,1:T(8,128)(2,1)S(1)}, u32[]{:S(2)}, u32[]{:S(2)}) async-start(bf16[1,8,16,512]{3,2,0,1:T(8,128)(2,1)} %bitcast.21), calls=%async_computation | async-start | bytes 262144 | tf_op jit(solution)/shard_map/all_to_all | solution.py:68
  67.8 5.3 %all-to-all-done = bf16[1,8,16,512]{3,2,0,1:T(8,128)(2,1)S(1)} async-done(((bf16[1,8,16,512]{3,2,0,1:T(8,128)(2,1)}), bf16[1,8,16,512]{3,2,0,1:T(8,128)(2,1)S(1)}, u32[]{:S(2)}, u32[]{:S(2)}) %all-to-all-start) | async-done | bytes 131104 | tf_op jit(solution)/shard_map/all_to_all | solution.py:68
  73.2 8.1 %multiply_add_fusion = f32[16,512,512]{2,1,0:T(8,128)} fusion(f32[512,512]{1,0:T(8,128)S(1)} %fusion.17, bf16[8,16,512]{2,1,0:T(8,128)(2,1)S(1)} %fusion.20), kind=kOutput, calls=%fused_computation.16 | convolution fusion | flops 75497472 | bytes 17956864 | tf_op jit(solution)/shard_map/nkc,nkd->kcd/dot_general | solution.py:46
  81.3 220.4 %while.10 = (s32[]{:T(128)}, bf16[16,512,512]{2,1,0:T(8,128)(2,1)}, f32[16,512,512]{2,1,0:T(8,128)}, s32[]{:T(128)}) while((s32[]{:T(128)}, bf16[16,512,512]{2,1,0:T(8,128)(2,1)}, f32[16,512,512]{2,1,0:T(8,128)}, s32[]{:T(128)}) %tuple.26), condition=%wide.region_3.4_spmd, body=%wide.region_1.3_spmd.sunk | while | flops 8056995840 | bytes 14681689 | solution.py:48
  86.4 3.1 fusion.76
  100.2 3.1 fusion.76
  114.0 3.1 fusion.76
  127.7 3.1 fusion.76
  141.5 3.1 fusion.76
  155.3 3.1 fusion.76
  169.0 3.1 fusion.76
  182.8 3.1 fusion.76
  196.6 3.1 fusion.76
  210.3 3.1 fusion.76
  224.1 3.1 fusion.76
  237.9 3.1 fusion.76
  251.7 3.1 fusion.76
  265.4 3.1 fusion.76
  279.2 3.1 fusion.76
  293.0 3.1 fusion.76
  301.7 4.6 %fusion.14 = bf16[8,1,16,512]{3,0,2,1:T(8,128)(2,1)S(1)} fusion(bf16[16,512,512]{2,1,0:T(8,128)(2,1)} %get-tuple-element.22, bf16[8,16,512]{2,1,0:T(8,128)(2,1)S(1)} %fusion.20), kind=kOutput, calls=%fused_computation.29 | convolution fusion | flops 67174400 | bytes 8650752 | tf_op jit(solution)/shard_map/nkc,kcd->nkd/dot_general | solution.py:50
  307.0 3.4 %all-to-all-start.1 = ((bf16[8,1,16,512]{3,2,1,0:T(8,128)(2,1)}), bf16[8,1,16,512]{3,2,1,0:T(8,128)(2,1)S(1)}, u32[]{:S(2)}, u32[]{:S(2)}) async-start(bf16[8,1,16,512]{3,2,1,0:T(8,128)(2,1)} %copy.11), calls=%async_computation.1 | async-start | bytes 262144 | tf_op jit(solution)/shard_map/all_to_all | solution.py:70
  310.4 5.4 %all-to-all-done.1 = bf16[8,1,16,512]{3,2,1,0:T(8,128)(2,1)S(1)} async-done(((bf16[8,1,16,512]{3,2,1,0:T(8,128)(2,1)}), bf16[8,1,16,512]{3,2,1,0:T(8,128)(2,1)S(1)}, u32[]{:S(2)}, u32[]{:S(2)}) %all-to-all-start.1) | async-done | bytes 131104 | tf_op jit(solution)/shard_map/all_to_all | solution.py:70
  (103 shorter events, 174.2 us)
Async XLA Ops:
  6.5 54.4 %copy-start = (bf16[1,16,8,512]{3,2,1,0:T(8,128)(2,1)S(1)}, bf16[1,16,8,512]{3,2,1,0:T(8,128)(2,1)}, u32[]{:S(2)}) copy-start(bf16[1,16,8,512]{3,2,1,0:T(8,128)(2,1)} %param.5) | copy-start | bytes 393220
  6.5 44.4 %all-gather.2.cloned.1.call-start = ((), (), s32[]{:S(2)}) async-start(), calls=%async_computation.2 | async-start | bytes 5308416 | tf_op jit(solution)/shard_map/all_gather | solution.py:63
  64.3 8.8 %all-to-all-start = ((bf16[1,8,16,512]{3,2,0,1:T(8,128)(2,1)}), bf16[1,8,16,512]{3,2,0,1:T(8,128)(2,1)S(1)}, u32[]{:S(2)}, u32[]{:S(2)}) async-start(bf16[1,8,16,512]{3,2,0,1:T(8,128)(2,1)} %bitcast.21), calls=%async_computation | async-start | bytes 262144 | tf_op jit(solution)/shard_map/all_to_all | solution.py:68
  301.7 8.7 %copy-start.1 = (f32[3,3,512]{2,1,0:T(4,128)S(1)}, f32[3,3,512]{2,1,0:T(4,128)}, u32[]{:S(2)}) copy-start(f32[3,3,512]{2,1,0:T(4,128)} %param.7) | copy-start | bytes 55300
  307.0 8.8 %all-to-all-start.1 = ((bf16[8,1,16,512]{3,2,1,0:T(8,128)(2,1)}), bf16[8,1,16,512]{3,2,1,0:T(8,128)(2,1)S(1)}, u32[]{:S(2)}, u32[]{:S(2)}) async-start(bf16[8,1,16,512]{3,2,1,0:T(8,128)(2,1)} %copy.11), calls=%async_computation.1 | async-start | bytes 262144 | tf_op jit(solution)/shard_map/all_to_all | solution.py:70
Sparse Core Ops, SparseCore 0:
  9.3 41.6 all-gather.1
where the time goes:
time: 326 us; the launch traced here: 323 us
  matrix products  200 us (61%)
  waiting for transfers between devices  55.1 us (17%)
  other arithmetic  34.6 us (11%)
  between operations  13.5 us (4%)
  loops' own time  12.3 us (4%)
  starting transfers between devices  6.75 us (2%)
    dot_general x32, matrix products, single_root(): product = jnp.dot(lower, upper, precision=lax.Precision.HIGHEST)  66.7 us
    dot_general x32, matrix products, single_root(): lower = jnp.dot(factor, lower, precision=lax.Precision.HIGHEST)  58.1 us
    dot_general x16, matrix products, single_root(): upper = jnp.dot(upper, factor, precision=lax.Precision.HIGHEST)  49.6 us
    all_gather x1, waiting for transfers between devices, shards(): kernel = lax.all_gather(conv_weight, 'dev', axis=3, tiled=True)  43.6 us
    reduce_sum x16, other arithmetic, single_root(): frob = jnp.sqrt(jnp.sum(moments * moments))  33.6 us
    dot_general x9, matrix products, convolve(): jnp.dot(flat_window, weights[row_tap, col_tap], preferred_element_type=jn...  13.3 us
    another operation x1, loops' own time, whiten_block(): roots = lax.map(single_root, moments)  12.3 us
    dot_general x1, matrix products, whiten_block(): jnp.einsum('nkc,nkd->kcd', centered, centered, preferred_element_type=jnp...  8.1 us
  transfers between devices with their start and end apart: 3, of which 3 were waited for; matrix products, arithmetic and copies ran while one was open for 0% of the time, Pallas kernels for 0%

commit v1 on v0

--- a/solution.py
+++ b/solution.py
@@ -1,9 +1,14 @@
+import functools
+
 import jax
 import jax.numpy as jnp
 from jax import lax
+from jax.experimental import pallas as pl
+from jax.experimental.pallas import tpu as pltpu
 from jax.sharding import PartitionSpec as P
 
 ITERS = 2
+MESH = pl.DeviceIdType.MESH
 
 
 ridge_term = 0.5
@@ -80,6 +85,321 @@
     return summed.astype(jnp.bfloat16)
 
 
+def flip(index, mask, bits):
+    flipped = 0
+    for bit in range(bits):
+        digit = (index // 2**bit) % 2
+        if (mask >> bit) & 1:
+            digit = 1 - digit
+        flipped = flipped + digit * 2**bit
+    return flipped
+
+
+def shift_lanes(values, step, keep):
+    lanes = values.shape[-1]
+    return jnp.where(keep, pltpu.roll(values, step % lanes, values.ndim - 1), 0.0)
+
+
+def small_product(left, right):
+    total = None
+    for k in range(right.shape[0]):
+        term = left[:, k : k + 1, :] * right[k : k + 1, :, :]
+        total = term if total is None else total + term
+    return total
+
+
+def fused_kernel(
+    grid_cols,
+    images,
+    channels,
+    x_in,
+    w_in,
+    smooth_in,
+    out_ref,
+    x_all,
+    w_own,
+    smooth_wide,
+    feats,
+    k_all,
+    mix,
+    sent,
+    local_sem,
+    x_send,
+    x_recv,
+    k_send,
+    k_recv,
+    o_send,
+    o_recv,
+):
+    bits = 3
+    me = lax.axis_index("dev")
+    positions = x_in.shape[0]
+    own = feats.shape[1]
+    half = positions // 2
+    peers = [flip(me, mask, bits) for mask in range(images)]
+
+    barrier = pltpu.get_barrier_semaphore()
+    for mask in range(1, images):
+        pl.semaphore_signal(
+            barrier, inc=1, device_id={"dev": peers[mask]}, device_id_type=MESH
+        )
+    load_x = pltpu.make_async_copy(x_in, x_all.at[me], local_sem.at[0])
+    load_w = pltpu.make_async_copy(w_in, w_own, local_sem.at[1])
+    load_x.start()
+    load_w.start()
+    pl.semaphore_wait(barrier, images - 1)
+
+    sends = []
+
+    def send_half(mask, part, to, from_input=False):
+        rows = pl.ds(part * half, half)
+        source = x_in.at[rows] if from_input else x_all.at[peers[mask], rows]
+        copy = pltpu.make_async_remote_copy(
+            src_ref=source,
+            dst_ref=x_all.at[peers[mask], rows],
+            send_sem=x_send.at[len(sends)],
+            recv_sem=x_recv.at[peers[mask], part],
+            device_id={"dev": peers[to]},
+            device_id_type=MESH,
+        )
+        copy.start()
+        sends.append(copy)
+
+    def await_half(mask, part):
+        rows = pl.ds(part * half, half)
+        pltpu.make_async_remote_copy(
+            src_ref=x_all.at[peers[mask], rows],
+            dst_ref=x_all.at[peers[mask], rows],
+            send_sem=x_send.at[0],
+            recv_sem=x_recv.at[peers[mask], part],
+            device_id={"dev": peers[1]},
+            device_id_type=MESH,
+        ).wait_recv()
+
+    send_half(0, 1, 2, True)
+    send_half(0, 0, 4, True)
+    send_half(0, 0, 2, True)
+    send_half(0, 1, 4, True)
+    send_half(0, 0, 1, True)
+    send_half(0, 1, 1, True)
+
+    per_group = 128 // own
+    group = pl.multiple_of((me // per_group) * 128, 128)
+    for row_tap in range(3):
+        for col_tap in range(3):
+            row = smooth_in[row_tap, pl.ds(col_tap, 1), pl.ds(group, 128)]
+            smooth_wide[row_tap * 3 + col_tap] = jnp.broadcast_to(row, (128, 128)).T
+    first = pl.multiple_of((me % per_group) * own, own)
+
+    lane = lax.broadcasted_iota(jnp.int32, (1, positions), 1)
+    keep_rows = [lane >= grid_cols, None, lane < positions - grid_cols]
+    keep_cols = [lane % grid_cols > 0, None, lane % grid_cols < grid_cols - 1]
+
+    def shift_row(values, tap):
+        return values if tap == 1 else shift_lanes(values, (1 - tap) * grid_cols, keep_rows[tap])
+
+    def shift_col(values, tap):
+        return values if tap == 1 else shift_lanes(values, 1 - tap, keep_cols[tap])
+
+    load_x.wait()
+    load_w.wait()
+
+    def convolve_pair(first_mask, second_mask):
+        pair = (peers[first_mask], peers[second_mask])
+        rows = jnp.concatenate([x_all[pair[0]], x_all[pair[1]]], axis=0)
+        taps = lax.dot_general(
+            w_own[...], rows, (((1,), (1,)), ((), ())), preferred_element_type=jnp.float32
+        )
+        for at in range(2):
+            total = None
+            for col_tap in range(3):
+                column = None
+                for row_tap in range(3):
+                    tap = row_tap * 3 + col_tap
+                    block = taps[tap * own : (tap + 1) * own, at * positions : (at + 1) * positions]
+                    block = shift_row(block, row_tap)
+                    column = block if column is None else column + block
+                column = shift_col(column, col_tap)
+                total = column if total is None else total + column
+            feats[pair[at]] = total.astype(jnp.bfloat16).astype(jnp.float32)
+
+    await_half(1, 0)
+    await_half(1, 1)
+    convolve_pair(0, 1)
+    await_half(4, 0)
+    send_half(4, 0, 2)
+    await_half(2, 1)
+    send_half(2, 1, 4)
+    send_half(4, 0, 1)
+    send_half(2, 1, 1)
+    await_half(2, 0)
+    send_half(2, 0, 1)
+    await_half(4, 1)
+    send_half(4, 1, 1)
+    convolve_pair(2, 4)
+    await_half(6, 0)
+    send_half(6, 0, 1)
+    await_half(6, 1)
+    send_half(6, 1, 1)
+    for mask in (3, 5):
+        await_half(mask, 0)
+        await_half(mask, 1)
+    convolve_pair(3, 5)
+    await_half(7, 0)
+    await_half(7, 1)
+    convolve_pair(6, 7)
+
+    center = feats[0]
+    for n in range(1, images):
+        center = center + feats[n]
+    center = center / images
+    for n in range(images):
+        feats[n] = (feats[n] - center).astype(jnp.bfloat16).astype(jnp.float32)
+    for n in range(images):
+        k_all[me, n] = jnp.sum(feats[n][None] * feats[...], axis=1)
+
+    k_sends = []
+    for mask in (6, 7, 2, 4, 3, 5, 1):
+        copy = pltpu.make_async_remote_copy(
+            src_ref=k_all.at[me],
+            dst_ref=k_all.at[me],
+            send_sem=k_send.at[mask],
+            recv_sem=k_recv.at[me],
+            device_id={"dev": peers[mask]},
+            device_id_type=MESH,
+        )
+        copy.start()
+        k_sends.append(copy)
+    for mask in range(1, images):
+        pltpu.make_async_remote_copy(
+            src_ref=k_all.at[peers[mask]],
+            dst_ref=k_all.at[peers[mask]],
+            send_sem=k_send.at[mask],
+            recv_sem=k_recv.at[peers[mask]],
+            device_id={"dev": peers[mask]},
+            device_id_type=MESH,
+        ).wait_recv()
+
+    shape = (images, images, positions)
+    diagonal = lax.broadcasted_iota(jnp.int32, shape, 0) == lax.broadcasted_iota(
+        jnp.int32, shape, 1
+    )
+    summed = k_all[0]
+    for source in range(1, images):
+        summed = summed + k_all[source]
+    moments = summed / (images - 1) + jnp.where(diagonal, ridge_term, 0.0)
+    squares = jnp.sum(jnp.sum(moments * moments, axis=0), axis=0, keepdims=True)
+    frob = jnp.sqrt(squares + ridge_term * ridge_term * (channels - images))[None]
+    upper = moments / frob
+    lower = None
+    for sweep in range(ITERS):
+        product = upper if lower is None else small_product(lower, upper)
+        factor = jnp.where(diagonal, 1.5, 0.0) - 0.5 * product
+        if sweep + 1 < ITERS:
+            upper = small_product(upper, factor)
+        lower = factor if lower is None else small_product(factor, lower)
+    mix[...] = lower / jnp.sqrt(frob)
+
+    o_sends = []
+    for mask in (6, 7, 2, 4, 3, 5, 1, 0):
+        target = peers[mask]
+        weights = mix[target]
+        white = None
+        for m in range(images):
+            term = weights[m : m + 1, :] * feats[m]
+            white = term if white is None else white + term
+        white = white.astype(jnp.bfloat16).astype(jnp.float32)
+        moved = [shift_col(white, col_tap) for col_tap in range(3)]
+        smoothed = None
+        for row_tap in range(3):
+            line = None
+            for col_tap in range(3):
+                term = moved[col_tap] * smooth_wide[row_tap * 3 + col_tap, pl.ds(first, own)]
+                line = term if line is None else line + term
+            line = shift_row(line, row_tap)
+            smoothed = line if smoothed is None else smoothed + line
+        sent[mask] = smoothed.astype(jnp.bfloat16)
+        if mask == 0:
+            keep = pltpu.make_async_copy(sent.at[0], out_ref.at[me], local_sem.at[0])
+            keep.start()
+        else:
+            copy = pltpu.make_async_remote_copy(
+                src_ref=sent.at[mask],
+                dst_ref=out_ref.at[me],
+                send_sem=o_send.at[mask],
+                recv_sem=o_recv.at[me],
+                device_id={"dev": target},
+                device_id_type=MESH,
+            )
+            copy.start()
+            o_sends.append(copy)
+    for copy in sends + k_sends:
+        copy.wait_send()
+    keep.wait()
+    for mask in range(1, images):
+        pltpu.make_async_remote_copy(
+            src_ref=sent.at[mask],
+            dst_ref=out_ref.at[peers[mask]],
+            send_sem=o_send.at[mask],
+            recv_sem=o_recv.at[peers[mask]],
+            device_id={"dev": peers[mask]},
+            device_id_type=MESH,
+        ).wait_recv()
+    for copy in o_sends:
+        copy.wait_send()
+
+
+def fused_shards(backbone, conv_weight, smooth_weight):
+    _, grid_rows, grid_cols, channels = backbone.shape
+    images = lax.axis_size("dev")
+    positions = grid_rows * grid_cols
+    own = conv_weight.shape[3]
+    x = backbone.reshape(positions, channels)
+    w = conv_weight.transpose(0, 1, 3, 2).reshape(9 * own, channels)
+    any_space = pl.BlockSpec(memory_space=pl.ANY)
+    vmem_space = pl.BlockSpec(memory_space=pltpu.VMEM)
+    gathered = pl.pallas_call(
+        functools.partial(fused_kernel, grid_cols, images, channels),
+        out_shape=jax.ShapeDtypeStruct((images, own, positions), jnp.bfloat16),
+        in_specs=[any_space, any_space, vmem_space],
+        out_specs=any_space,
+        scratch_shapes=[
+            pltpu.VMEM((images, positions, channels), jnp.bfloat16),
+            pltpu.VMEM((9 * own, channels), jnp.bfloat16),
+            pltpu.VMEM((9, 128, 128), jnp.float32),
+            pltpu.VMEM((images, own, positions), jnp.float32),
+            pltpu.VMEM((images, images, images, positions), jnp.float32),
+            pltpu.VMEM((images, images, positions), jnp.float32),
+            pltpu.VMEM((images, own, positions), jnp.bfloat16),
+            pltpu.SemaphoreType.DMA((2,)),
+            pltpu.SemaphoreType.DMA((14,)),
+            pltpu.SemaphoreType.DMA((images, 2)),
+            pltpu.SemaphoreType.DMA((images,)),
+            pltpu.SemaphoreType.DMA((images,)),
+            pltpu.SemaphoreType.DMA((images,)),
+            pltpu.SemaphoreType.DMA((images,)),
+        ],
+        compiler_params=pltpu.CompilerParams(
+            collective_id=0, has_side_effects=True, vmem_limit_bytes=24 * 2**20
+        ),
+    )(x, w, smooth_weight)
+    return gathered.reshape(channels, positions).T.reshape(backbone.shape)
+
+
+def choose_shards(backbone, conv_weight, smooth_weight):
+    local_images, grid_rows, grid_cols, _ = backbone.shape
+    own = conv_weight.shape[3]
+    fits = (
+        local_images == 1
+        and lax.axis_size("dev") == 2**3
+        and grid_rows * grid_cols == 128
+        and own % 16 == 0
+        and 128 % own == 0
+    )
+    form = fused_shards if fits else shards
+    return form(backbone, conv_weight, smooth_weight)
+
+
 def solution(mesh):
     placed = (
         P(("rep", "dev"), None, None, None),
@@ -87,7 +407,7 @@
         P(None, None, "rep"),
     )
     return jax.shard_map(
-        shards,
+        choose_shards,
         mesh=mesh,
         in_specs=placed,
         out_specs=P(("rep", "dev"), None, None, None),

time: 326 us -> 26 us (0.08)
  matrix products: 200 us -> 0 us
  waiting for transfers between devices: 55.1 us -> 0 us
  other arithmetic: 34.6 us -> 0 us
  Pallas kernels: 0 us -> 22.3 us
  between operations: 13.5 us -> 0.01 us
  loops' own time: 12.3 us -> 0 us
  starting transfers between devices: 6.75 us -> 0 us
    dot_general x91 -> x0, matrix products: 200 us -> none  [the longest x32 66.7 us: single_root(): product = jnp.dot(lower, upper, precision=lax.Precision.HIGHEST)]
    all_gather x1 -> x0, waiting for transfers between devices: 43.6 us -> none  [shards(): kernel = lax.all_gather(conv_weight, 'dev', axis=3, tiled=True)]
    reduce_sum x17 -> x0, other arithmetic: 33.6 us -> none  [the longest x16 33.6 us: single_root(): frob = jnp.sqrt(jnp.sum(moments * moments))]
    pallas_call x0 -> x1, Pallas kernels: none -> 22.3 us  [fused_shards(): pl.pallas_call(functools.partial(fused_kernel, grid_cols, images, channel...]
    another operation x1 -> x0, loops' own time: 12.3 us -> none  [whiten_block(): roots = lax.map(single_root, moments)]
    all_to_all x2 -> x0, waiting for transfers between devices: 10.8 us -> none  [the longest x1 5.43 us: shards(): lax.all_to_all(whitened, 'dev', split_axis=0, concat_axis=1, tiled=True)]
    all_to_all x2 -> x0, starting transfers between devices: 6.74 us -> none  [the longest x1 3.37 us: shards(): lax.all_to_all(features, 'dev', split_axis=1, concat_axis=0, tiled=True)]
  transfers between devices with their start and end apart: 3 -> 0, of which waited for: 3 -> 0; matrix products, arithmetic and copies ran while one was open for 0% -> 0% of each run, Pallas kernels for 0% -> 0%
where the time goes in v1:
time: 26 us; the launch traced here: 25.8 us
  Pallas kernels  22.3 us (86%)
  local copies, waits for them, and re-layouts  3.48 us (13%)
    pallas_call x1, Pallas kernels, fused_shards(): pl.pallas_call(functools.partial(fused_kernel, grid_cols, images, channel...  22.3 us
    unnamed x6, local copies, waits for them, and re-layouts  2.7 us
    transpose x1, local copies, waits for them, and re-layouts, fused_shards(): return gathered.reshape(channels, positions).T.reshape(backbone.shape)  0.77 us

profile of v1, /device:TPU:0, one launch (start us, length us, event | category | flops | bytes accessed | tf_op | source)
XLA Modules:
  0.0 25.8 jit_solution(6443648301648846833)
XLA Ops:
  0.0 0.0 copy-start
  0.0 1.1 %copy-done = bf16[3,3,512,64]{2,3,1,0:T(8,128)(2,1)S(1)} copy-done((bf16[3,3,512,64]{2,3,1,0:T(8,128)(2,1)S(1)}, bf16[3,3,512,64]{2,3,1,0:T(8,128)(2,1)}, u32[]{:S(2)}) %copy-start) | copy-done | bytes 589848
  1.1 0.0 copy-start.1
  1.1 0.9 %copy-done.1 = bf16[1,16,8,512]{3,2,1,0:T(8,128)(2,1)S(1)} copy-done((bf16[1,16,8,512]{3,2,1,0:T(8,128)(2,1)S(1)}, bf16[1,16,8,512]{3,2,1,0:T(8,128)(2,1)}, u32[]{:S(2)}) %copy-start.1) | copy-done | bytes 131096
  2.0 0.0 copy-start.2
  2.0 0.7 %copy-done.2 = f32[3,3,512]{2,1,0:T(4,128)S(1)} copy-done((f32[3,3,512]{2,1,0:T(4,128)S(1)}, f32[3,3,512]{2,1,0:T(4,128)}, u32[]{:S(2)}) %copy-start.2) | copy-done | bytes 18456
  2.7 22.3 %shard_map.37 = bf16[8,64,128]{2,1,0:T(8,128)(2,1)S(1)} custom-call(bf16[128,512]{1,0:T(8,128)(2,1)S(1)} %bitcast.10, bf16[576,512]{1,0:T(8,128)(2,1)S(1)} %bitcast.8, f32[3,3,512]{2,1,0:T(4,128)S(1)} %copy-done.2), custom_call_target="tpu_custom_call" | custom-call | tf_op jit(solution)/shard_map/pallas_call | solution.py:361
  25.0 0.8 %copy.4 = bf16[128,512]{1,0:T(8,128)(2,1)} copy(bf16[128,512]{0,1:T(8,128)(2,1)S(1)} %bitcast.9) | data formatting | bytes 262144 | tf_op jit(solution)/shard_map/transpose | solution.py:386
Async XLA Ops:
  0.0 1.1 %copy-start = (bf16[3,3,512,64]{2,3,1,0:T(8,128)(2,1)S(1)}, bf16[3,3,512,64]{2,3,1,0:T(8,128)(2,1)}, u32[]{:S(2)}) copy-start(bf16[3,3,512,64]{2,3,1,0:T(8,128)(2,1)} %param.4) | copy-start | bytes 1769476
  1.1 0.9 %copy-start.1 = (bf16[1,16,8,512]{3,2,1,0:T(8,128)(2,1)S(1)}, bf16[1,16,8,512]{3,2,1,0:T(8,128)(2,1)}, u32[]{:S(2)}) copy-start(bf16[1,16,8,512]{3,2,1,0:T(8,128)(2,1)} %param.3) | copy-start | bytes 393220
  2.0 0.7 %copy-start.2 = (f32[3,3,512]{2,1,0:T(4,128)S(1)}, f32[3,3,512]{2,1,0:T(4,128)}, u32[]{:S(2)}) copy-start(f32[3,3,512]{2,1,0:T(4,128)} %smooth_in.1) | copy-start | bytes 55300

commit v2 on v1

--- a/solution.py
+++ b/solution.py
@@ -9,6 +9,7 @@
 
 ITERS = 2
 MESH = pl.DeviceIdType.MESH
+PIECES = 2
 
 
 ridge_term = 0.5
@@ -100,14 +101,6 @@
     return jnp.where(keep, pltpu.roll(values, step % lanes, values.ndim - 1), 0.0)
 
 
-def small_product(left, right):
-    total = None
-    for k in range(right.shape[0]):
-        term = left[:, k : k + 1, :] * right[k : k + 1, :, :]
-        total = term if total is None else total + term
-    return total
-
-
 def fused_kernel(
     grid_cols,
     images,
@@ -118,6 +111,7 @@
     out_ref,
     x_all,
     w_own,
+    smooth_own,
     smooth_wide,
     feats,
     k_all,
@@ -135,7 +129,7 @@
     me = lax.axis_index("dev")
     positions = x_in.shape[0]
     own = feats.shape[1]
-    half = positions // 2
+    piece = positions // PIECES
     peers = [flip(me, mask, bits) for mask in range(images)]
 
     barrier = pltpu.get_barrier_semaphore()
@@ -145,14 +139,16 @@
         )
     load_x = pltpu.make_async_copy(x_in, x_all.at[me], local_sem.at[0])
     load_w = pltpu.make_async_copy(w_in, w_own, local_sem.at[1])
+    load_smooth = pltpu.make_async_copy(smooth_in, smooth_own, local_sem.at[2])
     load_x.start()
     load_w.start()
+    load_smooth.start()
     pl.semaphore_wait(barrier, images - 1)
 
     sends = []
 
-    def send_half(mask, part, to, from_input=False):
-        rows = pl.ds(part * half, half)
+    def send_piece(mask, part, to, from_input=False):
+        rows = pl.ds(part * piece, piece)
         source = x_in.at[rows] if from_input else x_all.at[peers[mask], rows]
         copy = pltpu.make_async_remote_copy(
             src_ref=source,
@@ -165,8 +161,8 @@
         copy.start()
         sends.append(copy)
 
-    def await_half(mask, part):
-        rows = pl.ds(part * half, half)
+    def await_piece(mask, part):
+        rows = pl.ds(part * piece, piece)
         pltpu.make_async_remote_copy(
             src_ref=x_all.at[peers[mask], rows],
             dst_ref=x_all.at[peers[mask], rows],
@@ -176,18 +172,27 @@
             device_id_type=MESH,
         ).wait_recv()
 
-    send_half(0, 1, 2, True)
-    send_half(0, 0, 4, True)
-    send_half(0, 0, 2, True)
-    send_half(0, 1, 4, True)
-    send_half(0, 0, 1, True)
-    send_half(0, 1, 1, True)
-
+    by_x = range(PIECES // 2)
+    by_y = range(PIECES // 2, PIECES)
+    for part in range(PIECES):
+        send_piece(0, part, 1, True)
+    for low, high in zip(by_x, by_y):
+        send_piece(0, high, 2, True)
+        send_piece(0, low, 4, True)
+    for copy in sends[PIECES:]:
+        copy.wait_send()
+    to_wait = sends[:PIECES]
+    already = len(sends)
+    for low, high in zip(by_x, by_y):
+        send_piece(0, low, 2, True)
+        send_piece(0, high, 4, True)
+
+    load_smooth.wait()
     per_group = 128 // own
     group = pl.multiple_of((me // per_group) * 128, 128)
     for row_tap in range(3):
         for col_tap in range(3):
-            row = smooth_in[row_tap, pl.ds(col_tap, 1), pl.ds(group, 128)]
+            row = smooth_own[row_tap, pl.ds(col_tap, 1), pl.ds(group, 128)]
             smooth_wide[row_tap * 3 + col_tap] = jnp.broadcast_to(row, (128, 128)).T
     first = pl.multiple_of((me % per_group) * own, own)
 
@@ -223,30 +228,33 @@
                 total = column if total is None else total + column
             feats[pair[at]] = total.astype(jnp.bfloat16).astype(jnp.float32)
 
-    await_half(1, 0)
-    await_half(1, 1)
+    for part in range(PIECES):
+        await_piece(1, part)
     convolve_pair(0, 1)
-    await_half(4, 0)
-    send_half(4, 0, 2)
-    await_half(2, 1)
-    send_half(2, 1, 4)
-    send_half(4, 0, 1)
-    send_half(2, 1, 1)
-    await_half(2, 0)
-    send_half(2, 0, 1)
-    await_half(4, 1)
-    send_half(4, 1, 1)
+    for low, high in zip(by_x, by_y):
+        await_piece(4, low)
+        send_piece(4, low, 2)
+        await_piece(2, high)
+        send_piece(2, high, 4)
+        send_piece(4, low, 1)
+        send_piece(2, high, 1)
+    for low, high in zip(by_x, by_y):
+        await_piece(2, low)
+        send_piece(2, low, 1)
+        await_piece(4, high)
+        send_piece(4, high, 1)
     convolve_pair(2, 4)
-    await_half(6, 0)
-    send_half(6, 0, 1)
-    await_half(6, 1)
-    send_half(6, 1, 1)
+    for low, high in zip(by_x, by_y):
+        await_piece(6, low)
+        send_piece(6, low, 1)
+        await_piece(6, high)
+        send_piece(6, high, 1)
     for mask in (3, 5):
-        await_half(mask, 0)
-        await_half(mask, 1)
+        for part in range(PIECES):
+            await_piece(mask, part)
     convolve_pair(3, 5)
-    await_half(7, 0)
-    await_half(7, 1)
+    for part in range(PIECES):
+        await_piece(7, part)
     convolve_pair(6, 7)
 
     center = feats[0]
@@ -255,8 +263,16 @@
     center = center / images
     for n in range(images):
         feats[n] = (feats[n] - center).astype(jnp.bfloat16).astype(jnp.float32)
-    for n in range(images):
-        k_all[me, n] = jnp.sum(feats[n][None] * feats[...], axis=1)
+    stored = images // 2 + 1
+    values = feats[...]
+    diagonals = []
+    for k in range(stored):
+        turned = values if k == 0 else jnp.concatenate([values[k:], values[:k]], axis=0)
+        diagonals.append(jnp.sum(values * turned, axis=1))
+    spare = k_all.shape[1] - stored * images
+    if spare:
+        diagonals.append(jnp.zeros((spare, positions), jnp.float32))
+    k_all[me] = jnp.concatenate(diagonals, axis=0).astype(k_all.dtype)
 
     k_sends = []
     for mask in (6, 7, 2, 4, 3, 5, 1):
@@ -280,33 +296,50 @@
             device_id_type=MESH,
         ).wait_recv()
 
-    shape = (images, images, positions)
-    diagonal = lax.broadcasted_iota(jnp.int32, shape, 0) == lax.broadcasted_iota(
-        jnp.int32, shape, 1
-    )
-    summed = k_all[0]
+    summed = k_all[0].astype(jnp.float32)
     for source in range(1, images):
-        summed = summed + k_all[source]
-    moments = summed / (images - 1) + jnp.where(diagonal, ridge_term, 0.0)
-    squares = jnp.sum(jnp.sum(moments * moments, axis=0), axis=0, keepdims=True)
-    frob = jnp.sqrt(squares + ridge_term * ridge_term * (channels - images))[None]
-    upper = moments / frob
+        summed = summed + k_all[source].astype(jnp.float32)
+
+    def complete(half):
+        return half + [pltpu.roll(half[images - k], images - k, 0) for k in range(stored, images)]
+
+    def product_of(left, right):
+        full_left, full_right = complete(left), complete(right)
+        result = []
+        for k in range(stored):
+            entry = None
+            for j in range(images):
+                other = full_right[(k - j) % images]
+                if j:
+                    other = pltpu.roll(other, images - j, 0)
+                term = full_left[j] * other
+                entry = term if entry is None else entry + term
+            result.append(entry)
+        return result
+
+    moments = [summed[k * images : (k + 1) * images] / (images - 1) for k in range(stored)]
+    moments[0] = moments[0] + ridge_term
+    squares = sum(entry * entry for entry in complete(moments))
+    squares = jnp.sum(squares, axis=0, keepdims=True)
+    frob = jnp.sqrt(squares + ridge_term * ridge_term * (channels - images))
+    upper = [entry / frob for entry in moments]
     lower = None
     for sweep in range(ITERS):
-        product = upper if lower is None else small_product(lower, upper)
-        factor = jnp.where(diagonal, 1.5, 0.0) - 0.5 * product
+        product = upper if lower is None else product_of(lower, upper)
+        factor = [-0.5 * entry for entry in product]
+        factor[0] = factor[0] + 1.5
         if sweep + 1 < ITERS:
-            upper = small_product(upper, factor)
-        lower = factor if lower is None else small_product(factor, lower)
-    mix[...] = lower / jnp.sqrt(frob)
+            upper = product_of(upper, factor)
+        lower = factor if lower is None else product_of(factor, lower)
+    for k, entry in enumerate(complete(lower)):
+        mix[k] = entry / jnp.sqrt(frob)
 
     o_sends = []
     for mask in (6, 7, 2, 4, 3, 5, 1, 0):
         target = peers[mask]
-        weights = mix[target]
         white = None
-        for m in range(images):
-            term = weights[m : m + 1, :] * feats[m]
+        for k in range(images):
+            term = mix[k, pl.ds(target, 1)] * feats[(target + k) % images]
             white = term if white is None else white + term
         white = white.astype(jnp.bfloat16).astype(jnp.float32)
         moved = [shift_col(white, col_tap) for col_tap in range(3)]
@@ -333,7 +366,7 @@
             )
             copy.start()
             o_sends.append(copy)
-    for copy in sends + k_sends:
+    for copy in to_wait + sends[already:] + k_sends:
         copy.wait_send()
     keep.wait()
     for mask in range(1, images):
@@ -356,31 +389,32 @@
     own = conv_weight.shape[3]
     x = backbone.reshape(positions, channels)
     w = conv_weight.transpose(0, 1, 3, 2).reshape(9 * own, channels)
-    any_space = pl.BlockSpec(memory_space=pl.ANY)
-    vmem_space = pl.BlockSpec(memory_space=pltpu.VMEM)
+    hbm_space = pl.BlockSpec(memory_space=pltpu.HBM)
+    packed = pl.cdiv((images // 2 + 1) * images, 16) * 16
     gathered = pl.pallas_call(
         functools.partial(fused_kernel, grid_cols, images, channels),
         out_shape=jax.ShapeDtypeStruct((images, own, positions), jnp.bfloat16),
-        in_specs=[any_space, any_space, vmem_space],
-        out_specs=any_space,
+        in_specs=[hbm_space] * 3,
+        out_specs=hbm_space,
         scratch_shapes=[
             pltpu.VMEM((images, positions, channels), jnp.bfloat16),
             pltpu.VMEM((9 * own, channels), jnp.bfloat16),
+            pltpu.VMEM(smooth_weight.shape, jnp.float32),
             pltpu.VMEM((9, 128, 128), jnp.float32),
             pltpu.VMEM((images, own, positions), jnp.float32),
-            pltpu.VMEM((images, images, images, positions), jnp.float32),
+            pltpu.VMEM((images, packed, positions), jnp.bfloat16),
             pltpu.VMEM((images, images, positions), jnp.float32),
             pltpu.VMEM((images, own, positions), jnp.bfloat16),
-            pltpu.SemaphoreType.DMA((2,)),
-            pltpu.SemaphoreType.DMA((14,)),
-            pltpu.SemaphoreType.DMA((images, 2)),
+            pltpu.SemaphoreType.DMA((3,)),
+            pltpu.SemaphoreType.DMA((7 * PIECES,)),
+            pltpu.SemaphoreType.DMA((images, PIECES)),
             pltpu.SemaphoreType.DMA((images,)),
             pltpu.SemaphoreType.DMA((images,)),
             pltpu.SemaphoreType.DMA((images,)),
             pltpu.SemaphoreType.DMA((images,)),
         ],
         compiler_params=pltpu.CompilerParams(
-            collective_id=0, has_side_effects=True, vmem_limit_bytes=24 * 2**20
+            collective_id=0, has_side_effects=True, vmem_limit_bytes=60 * 2**20
         ),
     )(x, w, smooth_weight)
     return gathered.reshape(channels, positions).T.reshape(backbone.shape)

time: 26 us -> 22.2 us (0.85)
  Pallas kernels: 22.3 us -> 20.3 us
  local copies, waits for them, and re-layouts: 3.48 us -> 1.67 us
    unnamed x6 -> x0, local copies, waits for them, and re-layouts: 2.7 us -> none
    pallas_call x1, Pallas kernels: 22.3 us -> 20.3 us  [fused_shards(): pl.pallas_call(functools.partial(fused_kernel, grid_cols, images, channel...]
    transpose x1, local copies, waits for them, and re-layouts: 0.77 us -> 1.67 us  [fused_shards(): return gathered.reshape(channels, positions).T.reshape(backbone.shape)]
where the time goes in v2:
time: 22.2 us; the launch traced here: 22 us
  Pallas kernels  20.3 us (91%)
  local copies, waits for them, and re-layouts  1.67 us (8%)
    pallas_call x1, Pallas kernels, fused_shards(): pl.pallas_call(functools.partial(fused_kernel, grid_cols, images, channel...  20.3 us
    transpose x1, local copies, waits for them, and re-layouts, fused_shards(): return gathered.reshape(channels, positions).T.reshape(backbone.shape)  1.67 us

profile of v2, /device:TPU:0, one launch (start us, length us, event | category | flops | bytes accessed | tf_op | source)
XLA Modules:
  0.0 22.0 jit_solution(7525678315728417124)
XLA Ops:
  0.0 20.3 %shard_map.37 = bf16[8,64,128]{2,1,0:T(8,128)(2,1)} custom-call(bf16[128,512]{1,0:T(8,128)(2,1)} %bitcast.10, bf16[576,512]{1,0:T(8,128)(2,1)} %bitcast.8, f32[3,3,512]{2,1,0:T(4,128)} %smooth_in.1), custom_call_target="tpu_custom_call" | custom-call | tf_op jit(solution)/shard_map/pallas_call | solution.py:394
  20.4 1.7 %copy.4 = bf16[128,512]{1,0:T(8,128)(2,1)} copy(bf16[128,512]{0,1:T(8,128)(2,1)} %bitcast.9) | data formatting | bytes 262144 | tf_op jit(solution)/shard_map/transpose | solution.py:420

commit v3 on v2

--- a/solution.py
+++ b/solution.py
@@ -209,13 +209,13 @@
     load_x.wait()
     load_w.wait()
 
-    def convolve_pair(first_mask, second_mask):
-        pair = (peers[first_mask], peers[second_mask])
-        rows = jnp.concatenate([x_all[pair[0]], x_all[pair[1]]], axis=0)
+    def convolve_group(*masks):
+        group = [peers[mask] for mask in masks]
+        rows = jnp.concatenate([x_all[at] for at in group], axis=0)
         taps = lax.dot_general(
             w_own[...], rows, (((1,), (1,)), ((), ())), preferred_element_type=jnp.float32
         )
-        for at in range(2):
+        for at in range(len(group)):
             total = None
             for col_tap in range(3):
                 column = None
@@ -226,11 +226,11 @@
                     column = block if column is None else column + block
                 column = shift_col(column, col_tap)
                 total = column if total is None else total + column
-            feats[pair[at]] = total.astype(jnp.bfloat16).astype(jnp.float32)
+            feats[group[at]] = total.astype(jnp.bfloat16).astype(jnp.float32)
 
     for part in range(PIECES):
         await_piece(1, part)
-    convolve_pair(0, 1)
+    convolve_group(0, 1)
     for low, high in zip(by_x, by_y):
         await_piece(4, low)
         send_piece(4, low, 2)
@@ -243,7 +243,7 @@
         send_piece(2, low, 1)
         await_piece(4, high)
         send_piece(4, high, 1)
-    convolve_pair(2, 4)
+    convolve_group(2, 4)
     for low, high in zip(by_x, by_y):
         await_piece(6, low)
         send_piece(6, low, 1)
@@ -252,10 +252,10 @@
     for mask in (3, 5):
         for part in range(PIECES):
             await_piece(mask, part)
-    convolve_pair(3, 5)
+    convolve_group(3, 5, 6)
     for part in range(PIECES):
         await_piece(7, part)
-    convolve_pair(6, 7)
+    convolve_group(7)
 
     center = feats[0]
     for n in range(1, images):

time: 22.2 us -> 22.1 us (level)
  no operation moved by 1% of the time
where the time goes in v3:
time: 22.1 us; the launch traced here: 22 us
  Pallas kernels  20.3 us (92%)
  local copies, waits for them, and re-layouts  1.67 us (8%)
    pallas_call x1, Pallas kernels, fused_shards(): pl.pallas_call(functools.partial(fused_kernel, grid_cols, images, channel...  20.3 us
    transpose x1, local copies, waits for them, and re-layouts, fused_shards(): return gathered.reshape(channels, positions).T.reshape(backbone.shape)  1.67 us

profile of v3, /device:TPU:0, one launch (start us, length us, event | category | flops | bytes accessed | tf_op | source)
XLA Modules:
  0.0 22.0 jit_solution(14477376473004789731)
XLA Ops:
  0.0 20.3 %shard_map.37 = bf16[8,64,128]{2,1,0:T(8,128)(2,1)} custom-call(bf16[128,512]{1,0:T(8,128)(2,1)} %bitcast.10, bf16[576,512]{1,0:T(8,128)(2,1)} %bitcast.8, f32[3,3,512]{2,1,0:T(4,128)} %smooth_in.1), custom_call_target="tpu_custom_call" | custom-call | tf_op jit(solution)/shard_map/pallas_call | solution.py:394
  20.3 1.7 %copy.4 = bf16[128,512]{1,0:T(8,128)(2,1)} copy(bf16[128,512]{0,1:T(8,128)(2,1)} %bitcast.9) | data formatting | bytes 262144 | tf_op jit(solution)/shard_map/transpose | solution.py:420
